TPU v7x, 512 devices: a whole 4x8x8 slice. The times are simulated.
512 devices in a mesh: sib: 2 (over core), row: 16 (over z_lo, y), col: 16 (over x, z_hi).
Axes of the slice: x: 4, y: 8, z: 8 (z_hi: 4, z_lo: 2; z = z_hi * 2 + z_lo), core: 2. Of those that a mesh axis runs over, the one named last changes fastest.
Arguments:
- child_pivot: bfloat16 [2, 384, 384], P('sib'), as said below
- child_border: bfloat16 [2, 12288, 384], P('sib', 'row')
- child_trailing: bfloat16 [2, 12288, 12288], P('sib', 'row', 'col'), as said below
- parent_pivot: bfloat16 [384, 384], replicated, as said below
- child_maps: int32 [2, 96], replicated, may hold values from 0 to 127, as said below
Outputs:
- parent_panel: bfloat16 [16384, 384], P('row')
- parent_update: bfloat16 [16384, 16384], P('row', ('sib', 'col'))
Inputs may be any that keep to these rules, and one draw needn't show every extreme that they name: `child_maps`: each row lists 96 different parent blocks in increasing order; every parent block appears in at least one of the two rows. Each child_pivot[s] is symmetric positive definite. Each child_trailing[s] is symmetric, and each child's whole front [[child_pivot[s], child_border[s]^T], [child_border[s], child_trailing[s]]] is positive definite. `parent_pivot`: symmetric positive definite.
All inputs are finite; a program needn't handle non-finite values.
Results may differ from a plain program's by a relative error of at most 0.01.
Values may be sent and summed in bfloat16 or wider, within the bound.
A program may use at most 64 MiB of HBM per device.

v0:
```python
import jax
import jax.numpy as jnp
from jax import lax
from jax.sharding import PartitionSpec as P

BLOCK = 128
PF = 16384


def from_root(block, axis, holder):
    block = jnp.where(lax.axis_index(axis) == holder, block, jnp.zeros_like(block))
    return lax.psum(block, axis)


def lower_solve(factor, rhs_rows):
    return jax.scipy.linalg.solve_triangular(factor, rhs_rows.T, lower=True).T


def outer_rows(left_rows, right_rows):
    return jnp.einsum("ik,jk->ij", left_rows, right_rows, preferred_element_type=jnp.float32)


def inverse_map(block_map, parent_blocks):
    child_blocks = block_map.shape[0]
    matches = block_map[:, None] == jnp.arange(parent_blocks, dtype=jnp.int32)[None, :]
    found_count = jnp.sum(matches.astype(jnp.int32), axis=0)
    source = jnp.sum(
        jnp.where(matches, jnp.arange(child_blocks, dtype=jnp.int32)[:, None], 0), axis=0
    )
    return jnp.where(found_count > 0, source, child_blocks)


def blocks_to_parent(values, inverse):
    leading = values.shape[0]
    block_tiles = values.reshape(leading, -1, BLOCK)
    zero_tile = jnp.zeros((leading, 1, BLOCK), values.dtype)
    widened = jnp.take(jnp.concatenate([block_tiles, zero_tile], axis=1), inverse, axis=1)
    return widened.reshape(leading, inverse.shape[0] * BLOCK)


def send_down(block, root):
    return from_root(block.astype(jnp.bfloat16), "row", root).astype(block.dtype)


def shards(child_pivot, child_border, child_trailing, parent_pivot, child_maps):
    row_count = lax.axis_size("row")
    col_count = lax.axis_size("col")
    sib_index = lax.axis_index("sib")
    row_index = lax.axis_index("row")
    col_index = lax.axis_index("col")
    pivot_count = parent_pivot.shape[0]
    factor = jnp.linalg.cholesky(child_pivot[0].astype(jnp.float32))
    own_panel = lower_solve(factor, child_border[0].astype(jnp.float32))
    other_panel = send_down(own_panel, col_index)
    own_short = own_panel.astype(jnp.bfloat16)
    other_short = other_panel.astype(jnp.bfloat16)
    schur_part = child_trailing[0].astype(jnp.float32) - outer_rows(own_short, other_short)
    update = schur_part.astype(jnp.bfloat16)
    block_map = lax.dynamic_index_in_dim(child_maps, sib_index, 0, keepdims=False)
    inverse = inverse_map(block_map, PF // BLOCK)
    row_strip = lax.all_to_all(update, "col", split_axis=0, concat_axis=1, tiled=True)
    spread = blocks_to_parent(row_strip, inverse)
    gathered = lax.all_to_all(
        lax.all_to_all(spread, "row", split_axis=1, concat_axis=0, tiled=True),
        "col",
        split_axis=1,
        concat_axis=0,
        tiled=True,
    )
    col_width = gathered.shape[1]
    strip_rows = row_strip.shape[0]
    natural = gathered.T.reshape(col_width, col_count, row_count, strip_rows)
    natural = natural.transpose(0, 2, 1, 3).reshape(col_width, -1)
    extended = blocks_to_parent(natural, inverse)
    tile_width = PF // (2 * col_count)
    pieces = extended.reshape(col_width, 2 * col_count, tile_width)
    pivot_part = jnp.broadcast_to(
        extended[:, None, :pivot_count], (col_width, 2 * col_count, pivot_count)
    )
    outgoing = jnp.concatenate([pieces, pivot_part], axis=2)
    arrived = lax.all_to_all(outgoing, ("sib", "col"), split_axis=1, concat_axis=0, tiled=True)
    halfway = arrived.shape[0] // 2
    summed = arrived[:halfway, 0].astype(jnp.float32) + arrived[halfway:, 0].astype(jnp.float32)
    front_tile = summed[:, :tile_width]
    pivot_columns = summed[:, tile_width:]
    anchor = parent_pivot.astype(jnp.float32)
    first_rows = row_index == 0
    at_corner = first_rows & (sib_index == 0) & (col_index == 0)
    front_tile = front_tile.at[:pivot_count, :pivot_count].add(jnp.where(at_corner, anchor, 0.0))
    pivot_columns = pivot_columns.at[:pivot_count, :].add(jnp.where(first_rows, anchor, 0.0))
    outgoing_rows = jnp.concatenate(
        [front_tile[:pivot_count, :].T, pivot_columns[:pivot_count, :]], axis=0
    )
    incoming = send_down(outgoing_rows, 0)
    cross_rows = incoming[:tile_width]
    pivot_block = incoming[tile_width:]
    parent_factor = jnp.linalg.cholesky(pivot_block)
    panel_rows = lower_solve(parent_factor, pivot_columns).astype(jnp.bfloat16)
    panel_cols = lower_solve(parent_factor, cross_rows).astype(jnp.bfloat16)
    schur_parent = front_tile - outer_rows(panel_rows, panel_cols)
    row_ids = row_index * front_tile.shape[0] + jnp.arange(front_tile.shape[0])
    col_ids = (sib_index * col_count + col_index) * tile_width + jnp.arange(tile_width)
    retained = (row_ids >= pivot_count)[:, None] & (col_ids >= pivot_count)[None, :]
    parent_update = jnp.where(retained, schur_parent, 0.0).astype(jnp.bfloat16)
    return (panel_rows, parent_update)


def solution(mesh):
    placed = (P("sib", None, None), P("sib", "row", None), P("sib", "row", "col"), P(), P())
    return jax.shard_map(
        shards,
        mesh=mesh,
        in_specs=placed,
        out_specs=(P("row", None), P("row", ("sib", "col"))),
        check_vma=False,
    )
```

profile of v0, /device:TPU:4, one launch (start us, length us, event | category | flops | bytes accessed | tf_op | source)
XLA Modules:
  0.0 786.2 jit_solution(22647912104438096)
XLA Ops:
  8.8 11.7 %cholesky.208 = f32[128,128]{1,0:T(8,128)S(1)} custom-call(f32[128,128]{1,0:T(8,128)S(1)} %cholesky.310), custom_call_target="Cholesky" | custom-call | tf_op jit(solution)/shard_map/jit(cholesky)/cholesky | solution.py:52
  20.5 9.8 %custom-call.29 = f32[1,128,128]{1,2,0:T(8,128)S(1)} custom-call(f32[1,128,128]{2,1,0:T(8,128)S(1)} %get-tuple-element.129), custom_call_target="InvertDiagBlocksLowerTriangular" | custom-call | tf_op jit(solution)/shard_map/jit(cholesky)/cholesky | solution.py:52
  31.1 11.7 %cholesky.227 = f32[128,128]{1,0:T(8,128)S(1)} custom-call(f32[128,128]{1,0:T(8,128)S(1)} %cholesky.314), custom_call_target="Cholesky" | custom-call | tf_op jit(solution)/shard_map/jit(cholesky)/cholesky | solution.py:52
  42.9 10.2 %custom-call.30 = f32[1,128,128]{1,2,0:T(8,128)S(1)} custom-call(f32[1,128,128]{2,1,0:T(8,128)S(1)} %get-tuple-element.127), custom_call_target="InvertDiagBlocksLowerTriangular" | custom-call | tf_op jit(solution)/shard_map/jit(cholesky)/cholesky | solution.py:52
  54.0 11.7 %cholesky.246 = f32[128,128]{1,0:T(8,128)S(1)} custom-call(f32[128,128]{1,0:T(8,128)S(1)} %convolution_subtract_fusion.9), custom_call_target="Cholesky" | custom-call | tf_op jit(solution)/shard_map/jit(cholesky)/cholesky | solution.py:52
  69.2 6.7 while.4
  69.9 1.4 dynamic-slice.28
  72.1 1.4 dynamic-slice.28
  74.3 1.4 dynamic-slice.28
  75.9 29.5 %custom-call.25 = f32[3,128,128]{1,2,0:T(8,128)S(1)} custom-call(f32[3,128,128]{2,1,0:T(8,128)S(1)} %get-tuple-element.34), custom_call_target="InvertDiagBlocksLowerTriangular" | custom-call | tf_op jit(solution)/shard_map/jit(_solve_triangular)/triangular_solve | solution.py:16
  109.3 146.2 %all-reduce.6.cloned.1.call-done = bf16[768,384]{0,1:T(8,128)(2,1)} async-done(((bf16[768,384]{0,1:T(8,128)(2,1)}), bf16[768,384]{0,1:T(8,128)(2,1)}) %all-reduce.6.cloned.1.call-update) | async-done | bytes 589840 | tf_op jit(solution)/shard_map/psum | solution.py:12
  255.5 2.9 fusion
  258.4 9.7 %all-to-all-start = ((bf16[16,48,768]{2,1,0:T(8,128)(2,1)}), bf16[16,48,768]{2,1,0:T(8,128)(2,1)S(1)}, u32[]{:S(2)}, u32[]{:S(2)}) async-start(bf16[16,48,768]{2,1,0:T(8,128)(2,1)} %bitcast.16), calls=%async_computation | async-start | bytes 2359296 | tf_op jit(solution)/shard_map/all_to_all | solution.py:61
  268.5 19.7 %all-to-all-done = bf16[16,48,768]{2,1,0:T(8,128)(2,1)S(1)} async-done(((bf16[16,48,768]{2,1,0:T(8,128)(2,1)}), bf16[16,48,768]{2,1,0:T(8,128)(2,1)S(1)}, u32[]{:S(2)}, u32[]{:S(2)}) %all-to-all-start) | async-done | bytes 1179680 | tf_op jit(solution)/shard_map/all_to_all | solution.py:61
  290.2 1.9 gather_fusion
  292.1 1.8 copy.132
  295.7 29.4 %all_to_all.63 = bf16[48,16,1024]{2,0,1:T(8,128)(2,1)} all-to-all(bf16[48,16,1024]{2,0,1:T(8,128)(2,1)S(1)} %copy.133), channel_id=1, replica_groups=mesh['sib'=2,'row'=16,'col'=16] {'row'}, dimensions={1} | all-to-all | bytes 3145728 | tf_op jit(solution)/shard_map/all_to_all | solution.py:64
  325.1 4.1 all_to_all.52
  329.2 3.4 copy.134
  332.6 13.8 %all-to-all-start.2 = ((bf16[768,16,64]{0,2,1:T(8,128)(2,1)}), bf16[768,16,64]{0,2,1:T(8,128)(2,1)S(1)}, u32[]{:S(2)}, u32[]{:S(2)}) async-start(bf16[768,16,64]{0,2,1:T(8,128)(2,1)} %copy.134), calls=%async_computation.2 | async-start | bytes 3145728 | tf_op jit(solution)/shard_map/all_to_all | solution.py:63
  346.7 29.7 %all-to-all-done.2 = bf16[768,16,64]{0,2,1:T(8,128)(2,1)S(1)} async-done(((bf16[768,16,64]{0,2,1:T(8,128)(2,1)}), bf16[768,16,64]{0,2,1:T(8,128)(2,1)S(1)}, u32[]{:S(2)}, u32[]{:S(2)}) %all-to-all-start.2) | async-done | bytes 1572896 | tf_op jit(solution)/shard_map/all_to_all | solution.py:63
  376.6 5.3 reshape.208
  381.9 5.2 copy.136
  387.1 7.0 reshape_reshape.4
  396.0 2.4 gather_fusion.1
  398.4 1.6 copy_bitcast_fusion
  400.0 2.6 copy.138
  402.6 3.1 gather.26
  407.3 3.1 copy.140
  410.3 7.9 %all-to-all-start.3 = ((bf16[64,32,896]{2,0,1:T(8,128)(2,1)}), bf16[64,32,896]{2,0,1:T(8,128)(2,1)}, u32[]{:S(2)}, u32[]{:S(2)}) async-start(bf16[64,32,896]{2,0,1:T(8,128)(2,1)} %copy.140), calls=%async_computation.3 | async-start | bytes 7340032 | tf_op jit(solution)/shard_map/all_to_all | solution.py:81
  419.4 80.9 %all-to-all-done.3 = bf16[64,32,896]{2,0,1:T(8,128)(2,1)} async-done(((bf16[64,32,896]{2,0,1:T(8,128)(2,1)}), bf16[64,32,896]{2,0,1:T(8,128)(2,1)}, u32[]{:S(2)}, u32[]{:S(2)}) %all-to-all-start.3) | async-done | bytes 3670048 | tf_op jit(solution)/shard_map/all_to_all | solution.py:81
  500.3 2.5 convert_add_fusion
  504.0 1.6 slice.228
  506.1 1.4 copy.158
  507.7 1.8 fusion.23
  513.4 142.4 %all-reduce.8.cloned.1.call-done = bf16[896,384]{0,1:T(8,128)(2,1)} async-done(((bf16[896,384]{0,1:T(8,128)(2,1)}), bf16[896,384]{0,1:T(8,128)(2,1)}) %all-reduce.8.cloned.1.call-update) | async-done | bytes 688144 | tf_op jit(solution)/shard_map/psum | solution.py:12
  660.0 11.7 %cholesky.261 = f32[128,128]{1,0:T(8,128)S(1)} custom-call(f32[128,128]{1,0:T(8,128)S(1)} %cholesky.318), custom_call_target="Cholesky" | custom-call | tf_op jit(solution)/shard_map/jit(cholesky)/cholesky | solution.py:97
  671.8 9.8 %custom-call.31 = f32[1,128,128]{1,2,0:T(8,128)S(1)} custom-call(f32[1,128,128]{2,1,0:T(8,128)S(1)} %get-tuple-element.125), custom_call_target="InvertDiagBlocksLowerTriangular" | custom-call | tf_op jit(solution)/shard_map/jit(cholesky)/cholesky | solution.py:97
  684.0 12.1 %cholesky.280 = f32[128,128]{1,0:T(8,128)S(1)} custom-call(f32[128,128]{1,0:T(8,128)S(1)} %cholesky.322), custom_call_target="Cholesky" | custom-call | tf_op jit(solution)/shard_map/jit(cholesky)/cholesky | solution.py:97
  696.4 9.8 %custom-call.32 = f32[1,128,128]{1,2,0:T(8,128)S(1)} custom-call(f32[1,128,128]{2,1,0:T(8,128)S(1)} %get-tuple-element.123), custom_call_target="InvertDiagBlocksLowerTriangular" | custom-call | tf_op jit(solution)/shard_map/jit(cholesky)/cholesky | solution.py:97
  709.3 1.4 convolution_subtract_fusion.8
  710.7 11.7 %cholesky.299 = f32[128,128]{1,0:T(8,128)S(1)} custom-call(f32[128,128]{1,0:T(8,128)S(1)} %convolution_subtract_fusion.8), custom_call_target="Cholesky" | custom-call | tf_op jit(solution)/shard_map/jit(cholesky)/cholesky | solution.py:97
  729.1 6.3 while.5
  735.4 29.5 %custom-call.26 = f32[3,128,128]{1,2,0:T(8,128)S(1)} custom-call(f32[3,128,128]{2,1,0:T(8,128)S(1)} %get-tuple-element.42), custom_call_target="InvertDiagBlocksLowerTriangular" | custom-call | tf_op jit(solution)/shard_map/jit(_solve_triangular)/triangular_solve | solution.py:16
  765.9 1.4 convolution_subtract_fusion.5
  768.4 1.4 convolution_subtract_fusion.4
  770.2 1.5 fusion.71
  776.3 2.8 select_convert_fusion
  (172 shorter events, 53.4 us)
Async XLA Ops:
  7.2 261.0 %copy-start = (s32[2,96]{1,0:T(2,128)S(1)}, s32[2,96]{1,0:T(2,128)}, u32[]{:S(2)}) copy-start(s32[2,96]{1,0:T(2,128)} %param.14) | copy-start | bytes 2308
  7.2 248.3 %all-reduce.6.cloned.1.call-start = ((), (), s32[]{:S(2)}) async-start(), calls=%async_computation.4 | async-start | bytes 1179648 | tf_op jit(solution)/shard_map/psum | solution.py:12
  69.1 36.3 %copy-start.11 = (bf16[1,768,384]{2,1,0:T(8,128)(2,1)S(1)}, bf16[1,768,384]{2,1,0:T(8,128)(2,1)}, u32[]{:S(2)}) copy-start(bf16[1,768,384]{2,1,0:T(8,128)(2,1)} %param.11) | copy-start | bytes 1769476
  107.8 147.7 %copy-start.13 = (bf16[1,768,768]{2,1,0:T(8,128)(2,1)S(1)}, bf16[1,768,768]{2,1,0:T(8,128)(2,1)}, u32[]{:S(2)}) copy-start(bf16[1,768,768]{2,1,0:T(8,128)(2,1)} %param.12) | copy-start | bytes 3538948
  258.4 29.8 %all-to-all-start = ((bf16[16,48,768]{2,1,0:T(8,128)(2,1)}), bf16[16,48,768]{2,1,0:T(8,128)(2,1)S(1)}, u32[]{:S(2)}, u32[]{:S(2)}) async-start(bf16[16,48,768]{2,1,0:T(8,128)(2,1)} %bitcast.16), calls=%async_computation | async-start | bytes 2359296 | tf_op jit(solution)/shard_map/all_to_all | solution.py:61
  332.6 43.9 %all-to-all-start.2 = ((bf16[768,16,64]{0,2,1:T(8,128)(2,1)}), bf16[768,16,64]{0,2,1:T(8,128)(2,1)S(1)}, u32[]{:S(2)}, u32[]{:S(2)}) async-start(bf16[768,16,64]{0,2,1:T(8,128)(2,1)} %copy.134), calls=%async_computation.2 | async-start | bytes 3145728 | tf_op jit(solution)/shard_map/all_to_all | solution.py:63
  410.3 8.2 %copy-start.12 = (bf16[384,384]{1,0:T(8,128)(2,1)S(1)}, bf16[384,384]{1,0:T(8,128)(2,1)}, u32[]{:S(2)}) copy-start(bf16[384,384]{1,0:T(8,128)(2,1)} %param.13) | copy-start | bytes 884740
  410.3 90.0 %all-to-all-start.3 = ((bf16[64,32,896]{2,0,1:T(8,128)(2,1)}), bf16[64,32,896]{2,0,1:T(8,128)(2,1)}, u32[]{:S(2)}, u32[]{:S(2)}) async-start(bf16[64,32,896]{2,0,1:T(8,128)(2,1)} %copy.140), calls=%async_computation.3 | async-start | bytes 7340032 | tf_op jit(solution)/shard_map/all_to_all | solution.py:81
  418.2 237.6 %all-reduce.8.cloned.1.call-start = ((), (), s32[]{:S(2)}) async-start(), calls=%async_computation.5 | async-start | bytes 1376256 | tf_op jit(solution)/shard_map/psum | solution.py:12
  506.1 1.4 copy-start.5
  509.5 2.3 copy-start.7
  657.9 1.3 copy-start.4
  659.2 0.8 copy-start.6
  727.8 37.0 %copy-start.2 = (bf16[896,384]{0,1:T(8,128)(2,1)S(1)}, bf16[896,384]{0,1:T(8,128)(2,1)}, u32[]{:S(2)}) copy-start(bf16[896,384]{0,1:T(8,128)(2,1)} %all-reduce.8.cloned.1.call-done) | copy-start | bytes 2064388
  764.9 4.9 copy-start.9
  770.2 2.2 copy-start.10
  773.0 1.4 copy-start.8
  774.4 1.9 copy-start.3
  774.4 1.9 copy-start.14
  776.3 2.8 copy-start.1
Sparse Core Ops, SparseCore 0:
  109.4 146.0 all-reduce.5
  513.0 142.8 all-reduce.7
where the time goes:
time: 796 us; the launch traced here: 786 us
  waiting for transfers between devices  419 us (53%)
  other arithmetic  184 us (23%)
  local copies, waits for them, and re-layouts  79.4 us (10%)
  starting transfers between devices  31.7 us (4%)
  blocking collectives  29.4 us (4%)
  matrix products  23.5 us (3%)
  between operations  18.8 us (2%)
    psum x2, waiting for transfers between devices, from_root(): return lax.psum(block, axis)  289 us
    all_to_all x1, waiting for transfers between devices, shards(): lax.all_to_all(outgoing, ('sib', 'col'), split_axis=1, concat_axis=0, til...  80.9 us
    another operation x5, other arithmetic, lower_solve(): return jax.scipy.linalg.solve_triangular(factor, rhs_rows.T, lower=True).T  60.2 us
    another operation x11, other arithmetic, shards(): parent_factor = jnp.linalg.cholesky(pivot_block)  57.2 us
    another operation x10, other arithmetic, shards(): factor = jnp.linalg.cholesky(child_pivot[0].astype(jnp.float32))  56.6 us
    all_to_all x1, waiting for transfers between devices, shards(): lax.all_to_all(lax.all_to_all(spread, 'row', split_axis=1, concat_axis=0,...  29.7 us
    all_to_all x1, blocking collectives, shards(): lax.all_to_all(spread, 'row', split_axis=1, concat_axis=0, tiled=True)  29.4 us
    all_to_all x1, waiting for transfers between devices, shards(): lax.all_to_all(update, 'col', split_axis=0, concat_axis=1, tiled=True)  19.7 us
  transfers between devices with their start and end apart: 5, of which 5 were waited for; matrix products, arithmetic and copies ran while one was open for 0% of the time, Pallas kernels for 0%

commit v1 on v0

v1 whole, which is shorter than its diff:
```python
import jax
import jax.numpy as jnp
from jax import lax
from jax.experimental import pallas as pl
from jax.experimental.pallas import tpu as pltpu
from jax.sharding import PartitionSpec as P

BF16 = jnp.bfloat16
F32 = jnp.float32
HIGHEST = lax.Precision.HIGHEST
NT = (((1,), (1,)), ((), ()))
MESH = pl.DeviceIdType.MESH
ROWS = 16
COLS = 16


def mm(a, b):
    return jnp.dot(a, b, precision=HIGHEST, preferred_element_type=F32)


def mm_nt(a, b):
    return lax.dot_general(a, b, NT, precision=HIGHEST, preferred_element_type=F32)


def dot_nt(a, b):
    return lax.dot_general(a, b, NT, preferred_element_type=F32)


def block_inverse(s_ref, i_ref):
    n = 128
    rows = lax.broadcasted_iota(jnp.int32, (n, n), 0)
    cols = lax.broadcasted_iota(jnp.int32, (n, n), 1)
    x = s_ref[...]
    m = jnp.where(rows == cols, 1.0, 0.0)
    for panel in range(n // 8):
        for o in range(0, 8, 4):
            j = 8 * panel + o
            w = [jnp.broadcast_to(x[:, j + k:j + k + 1], x.shape) for k in range(4)]
            g = [[w[q][o + p:o + p + 1, :] for q in range(4)] for p in range(4)]
            xr = [x[o + k:o + k + 1, :] for k in range(4)]
            mr = [m[o + k:o + k + 1, :] for k in range(4)]
            a, b, c = g[0][0], g[1][0], g[1][1]
            inv = 1.0 / (a * c - b * b)
            ci, bi, ai = c * inv, b * inv, a * inv
            def pair(r1, r2, ci=ci, bi=bi, ai=ai):
                return ci * r1 - bi * r2, ai * r2 - bi * r1
            x1p, x2p = pair(xr[0], xr[1])
            m1p, m2p = pair(mr[0], mr[1])
            i_ref[j:j + 1, :] = mr[0] * lax.rsqrt(a)
            i_ref[j + 1:j + 2, :] = m2p * lax.rsqrt(ai)
            p20, p21 = pair(g[2][0], g[2][1])
            p30, p31 = pair(g[3][0], g[3][1])
            a2 = g[2][2] - (g[2][0] * p20 + g[2][1] * p21)
            b2 = g[3][2] - (g[3][0] * p20 + g[3][1] * p21)
            c2 = g[3][3] - (g[3][0] * p30 + g[3][1] * p31)
            inv2 = 1.0 / (a2 * c2 - b2 * b2)
            ci2, bi2, ai2 = c2 * inv2, b2 * inv2, a2 * inv2
            x3 = xr[2] - g[2][0] * x1p - g[2][1] * x2p
            x4 = xr[3] - g[3][0] * x1p - g[3][1] * x2p
            m3 = mr[2] - g[2][0] * m1p - g[2][1] * m2p
            m4 = mr[3] - g[3][0] * m1p - g[3][1] * m2p
            x3p, x4p = pair(x3, x4, ci2, bi2, ai2)
            m3p, m4p = pair(m3, m4, ci2, bi2, ai2)
            i_ref[j + 2:j + 3, :] = m3 * lax.rsqrt(a2)
            i_ref[j + 3:j + 4, :] = m4p * lax.rsqrt(ai2)
            if o == 4:
                x, m = x[8:, :], m[8:, :]
                w = [t[8:, :] for t in w]
                if panel == n // 8 - 1:
                    break
            f1, f2 = pair(w[0], w[1])
            u3 = w[2] - f1 * g[2][0] - f2 * g[2][1]
            u4 = w[3] - f1 * g[3][0] - f2 * g[3][1]
            x = x - w[0] * x1p - w[1] * x2p - u3 * x3p - u4 * x4p
            m = m - w[0] * m1p - w[1] * m2p - u3 * m3p - u4 * m4p


def factor_inverse(a_ref, out_ref, s_ref, i_ref, l_ref):
    n = 384
    a = a_ref[...]
    rows = lax.broadcasted_iota(jnp.int32, (n, n), 0)
    cols = lax.broadcasted_iota(jnp.int32, (n, n), 1)
    diag = jnp.where(rows == cols, a, 0.0)
    dr = lax.rsqrt(jnp.sum(diag, axis=0, keepdims=True))
    dc = lax.rsqrt(jnp.sum(diag, axis=1, keepdims=True))
    a_ref[...] = a * dr * dc
    b = [pl.ds(128 * k, 128) for k in range(3)]
    out_ref[...] = jnp.zeros((n, n), F32)
    s_ref[...] = a_ref[b[0], b[0]]

    def body(k, carry):
        block_inverse(s_ref, i_ref)
        inv = i_ref[...]

        @pl.when(k == 0)
        def _():
            out_ref[b[0], b[0]] = inv
            l21 = mm_nt(a_ref[b[1], b[0]], inv)
            s_ref[...] = a_ref[b[1], b[1]] - mm_nt(l21, l21)
            l31 = mm_nt(a_ref[b[2], b[0]], inv)
            a_ref[b[2], b[1]] = a_ref[b[2], b[1]] - mm_nt(l31, l21)
            a_ref[b[2], b[2]] = a_ref[b[2], b[2]] - mm_nt(l31, l31)
            l_ref[0] = mm(l21, inv)
            l_ref[1] = mm(l31, inv)

        @pl.when(k == 1)
        def _():
            out_ref[b[1], b[1]] = inv
            l32 = mm_nt(a_ref[b[2], b[1]], inv)
            s_ref[...] = a_ref[b[2], b[2]] - mm_nt(l32, l32)
            x21 = -mm(inv, l_ref[0])
            out_ref[b[1], b[0]] = x21
            l_ref[1] = l_ref[1] + mm(l32, x21)
            l_ref[2] = mm(l32, inv)

        @pl.when(k == 2)
        def _():
            out_ref[b[2], b[2]] = inv
            out_ref[b[2], b[0]] = -mm(inv, l_ref[1])
            out_ref[b[2], b[1]] = -mm(inv, l_ref[2])

        return carry

    lax.fori_loop(0, 3, body, 0)
    out_ref[...] = out_ref[...] * dr


FACTOR_SCRATCH = [
    pltpu.VMEM((384, 384), F32),
    pltpu.VMEM((128, 128), F32),
    pltpu.VMEM((128, 128), F32),
    pltpu.VMEM((3, 128, 128), F32),
]


def child_kernel(pivot_ref, out_ref, a_ref, s_ref, i_ref, l_ref):
    a_ref[...] = pivot_ref[...].astype(F32)
    factor_inverse(a_ref, out_ref, s_ref, i_ref, l_ref)


def child_inverse(pivot):
    return pl.pallas_call(
        child_kernel,
        out_shape=jax.ShapeDtypeStruct((384, 384), F32),
        in_specs=[pl.BlockSpec(memory_space=pltpu.VMEM)],
        out_specs=pl.BlockSpec(memory_space=pltpu.VMEM),
        scratch_shapes=FACTOR_SCRATCH,
        compiler_params=pltpu.CompilerParams(vmem_limit_bytes=32 << 20),
        cost_estimate=pl.CostEstimate(flops=2 * 10**9, bytes_accessed=10**6, transcendentals=0),
    )(pivot)


def panel_of(border, inverse):
    high = inverse.astype(BF16)
    rest = inverse - high.astype(F32)
    middle = rest.astype(BF16)
    low = (rest - middle.astype(F32)).astype(BF16)
    return (dot_nt(border, high) + (dot_nt(border, middle) + dot_nt(border, low))).astype(BF16)


def front_kernel(
    maps_ref, trailing_ref, border_ref, cross_ref, inverse_ref, pivot_ref,
    panel_ref, update_ref,
    pr, pc, u, z1, w1, v, z3, xs, xr, fs, fr, y, z4, prow, pcol, crn, parent_inv,
    a_ref, s_ref, i_ref, l_ref,
    z1s, z1r, z2s, z2r, z3s, z3r, z4s, z4r, g1s, g1r, g2s, g2r,
    cas, car, cbs, cbr, ccs, ccr, sws, swr, xss, xsr, lsem,
):
    s = lax.axis_index("sib")
    r = lax.axis_index("row")
    c = lax.axis_index("col")
    other = 1 - s
    g, h = r // 2, r % 2

    sends_cols = s == r // 8
    cols_to = 2 * (r % 8) + c // 8
    cols_from_row = 8 * s + c // 2
    cols_from_col = 8 * (c % 2)

    def remote(src, dst, send, recv, **to):
        return pltpu.make_async_remote_copy(
            src_ref=src, dst_ref=dst, send_sem=send, recv_sem=recv, device_id=to, device_id_type=MESH
        )

    def each(first, last, body):
        def step(k, carry):
            body(k)
            return carry
        lax.fori_loop(first, last, step, 0)

    barrier = pltpu.get_barrier_semaphore()

    def greet(j):
        pl.semaphore_signal(barrier, inc=1, device_id={"row": lax.rem(r + j, ROWS)}, device_id_type=MESH)
        pl.semaphore_signal(barrier, inc=1, device_id={"col": lax.rem(c + j, COLS)}, device_id_type=MESH)

    each(1, 16, greet)
    pl.semaphore_signal(barrier, inc=1, device_id={"sib": other}, device_id_type=MESH)

    def greet_cols(k):
        @pl.when(jnp.logical_not((cols_from_row == r) & (cols_from_col + k == c)))
        def _():
            pl.semaphore_signal(
                barrier, inc=1, device_id={"row": cols_from_row, "col": cols_from_col + k}, device_id_type=MESH
            )

    each(0, 8, greet_cols)

    inverse = inverse_ref[...]
    pr[...] = panel_of(border_ref[...], inverse)
    pc[...] = panel_of(cross_ref[...], inverse)
    for i in range(6):
        rows = pl.ds(128 * i, 128)
        value = trailing_ref[rows, :].astype(F32) - dot_nt(pr[rows, :], pc[...])
        value = value.astype(BF16)
        for q in range(6):
            u[q, i] = value[:, 128 * q:128 * (q + 1)].reshape(8, 16, 128)

    expected = 31 + jnp.where(sends_cols, 16 - (cols_to == c).astype(jnp.int32), 0)
    pl.semaphore_wait(barrier, expected)

    at_root = (r == 0) & (c == 0)
    holds = r < 8

    def corner_a(k):
        return remote(u.at[0:3, 0:3, k], crn.at[s, :, :, k], cas.at[k], car.at[0], row=k)

    @pl.when(at_root)
    def _():
        each(1, 8, lambda k: corner_a(k).start())
        own = pltpu.make_async_copy(u.at[0:3, 0:3, 0], crn.at[s, :, :, 0], lsem.at[0])
        own.start()
        own.wait()

    def first(k):
        return remote(
            u.at[pl.ds(3 * (k % 2), 3), :, k // 2], z1.at[:, pl.ds(6 * r, 6)], z1s.at[k], z1r.at[r], row=k
        )

    def first_from(k):
        return remote(
            u.at[pl.ds(3 * h, 3), :, g], z1.at[:, pl.ds(6 * k, 6)], z1s.at[k], z1r.at[k], row=k
        )

    each(1, 16, lambda j: first(lax.rem(r + j, ROWS)).start())
    own1 = pltpu.make_async_copy(u.at[pl.ds(3 * h, 3), :, g], z1.at[:, pl.ds(6 * r, 6)], lsem.at[1])
    own1.start()
    z1[:, 96] = jnp.zeros((3, 16, 128), BF16)
    z3[96] = jnp.zeros((4, 16, 128), BF16)
    own1.wait()

    def corner_b(k):
        return remote(crn.at[s, :, :, r], crn.at[s, :, :, r], cbs.at[k], cbr.at[0], col=k)

    @pl.when(holds & (c == 0))
    def _():
        @pl.when(r > 0)
        def _():
            corner_a(r).wait_recv()
        each(1, 16, lambda k: corner_b(k).start())

    each(1, 16, lambda j: first_from(lax.rem(r + j, ROWS)).wait_recv())

    def second(k):
        return remote(
            w1.at[:, pl.ds(8 * k, 8)], v.at[pl.ds(3 * h, 3), :, g], z2s.at[k], z2r.at[r], row=k
        )

    def second_from(k):
        return remote(
            w1.at[:, pl.ds(8 * r, 8)], v.at[pl.ds(3 * (k % 2), 3), :, k // 2], z2s.at[k], z2r.at[k], row=k
        )

    def widen_rows(k):
        for j in range(8):
            p = 8 * k + j
            w1[:, p] = z1[:, maps_ref[s, p]]

    def send_second(j):
        k = lax.rem(r + j, ROWS)
        widen_rows(k)
        second(k).start()

    each(1, 16, send_second)
    widen_rows(r)
    own2 = pltpu.make_async_copy(w1.at[:, pl.ds(8 * r, 8)], v.at[pl.ds(3 * h, 3), :, g], lsem.at[2])
    own2.start()

    def corner_c(k):
        return remote(crn.at[s, :, :, r], crn.at[s, :, :, r], ccs.at[k], ccr.at[r], row=k)

    def corner_c_from(k):
        return remote(crn.at[s, :, :, k], crn.at[s, :, :, k], ccs.at[k], ccr.at[k], row=k)

    @pl.when(holds)
    def _():
        @pl.when(c > 0)
        def _():
            corner_b(c).wait_recv()
        each(1, 16, lambda j: corner_c(lax.rem(r + j, ROWS)).start())

    own2.wait()
    each(1, 16, lambda j: second_from(lax.rem(r + j, ROWS)).wait_recv())

    def third(k):
        return remote(
            v.at[:, k // 2, pl.ds(4 * (k % 2), 4)], z3.at[pl.ds(6 * c, 6)], z3s.at[k], z3r.at[c], col=k
        )

    def third_from(k):
        return remote(
            v.at[:, c // 2, pl.ds(4 * (c % 2), 4)], z3.at[pl.ds(6 * k, 6)], z3s.at[k], z3r.at[k], col=k
        )
    each(1, 16, lambda j: third(lax.rem(c + j, COLS)).start())
    own3 = pltpu.make_async_copy(
        v.at[:, c // 2, pl.ds(4 * (c % 2), 4)], z3.at[pl.ds(6 * c, 6)], lsem.at[3]
    )
    own3.start()

    def corner_rest(k):
        @pl.when(k != r)
        def _():
            corner_c_from(k).wait_recv()

    each(0, 8, corner_rest)
    swap = remote(crn.at[s], crn.at[s], sws.at[0], swr.at[0], sib=other)
    swap_back = remote(crn.at[s], crn.at[other], sws.at[0], swr.at[0], sib=other)
    swap.start()
    swap_back.wait_recv()
    for p in range(3):
        for q in range(3):
            total = pivot_ref[128 * p:128 * (p + 1), 128 * q:128 * (q + 1)].astype(F32)
            for child in range(2):
                i, j = maps_ref[child, p], maps_ref[child, q]
                present = (i < 3) & (j < 3)
                block = crn[child, jnp.minimum(j, 2), jnp.minimum(i, 2)].astype(F32).reshape(128, 128)
                total = total + jnp.where(present, block, 0.0)
            a_ref[128 * p:128 * (p + 1), 128 * q:128 * (q + 1)] = total
    factor_inverse(a_ref, parent_inv, s_ref, i_ref, l_ref)

    own3.wait()
    each(1, 16, lambda j: third_from(lax.rem(c + j, COLS)).wait_recv())

    def strip(p):
        return z3[maps_ref[s, p]]

    for p in range(3):
        fs[p] = strip(p)
    swap_pivots = remote(fs, fr, sws.at[1], swr.at[1], sib=other)
    swap_pivots.start()

    def half(k):
        return remote(xs.at[pl.ds(4 * k, 4)], xr.at[pl.ds(4 * k, 4)], xss.at[k], xsr.at[k], sib=other)

    def send_half(j):
        k = lax.rem(c + j, COLS)
        for q in range(4):
            xs[4 * k + q] = strip(64 * other + 4 * k + q)
        half(k).start()

    each(1, 17, send_half)

    swap_pivots.wait_recv()
    first_rows = (r == 0) & (c < 6)
    start_row = pl.multiple_of(64 * jnp.minimum(c, 5), 64)
    anchor = jnp.where(first_rows, pivot_ref[pl.ds(start_row, 64), :].astype(F32), 0.0)
    rows = jnp.concatenate(
        [fs[p].astype(F32).reshape(64, 128) + fr[p].astype(F32).reshape(64, 128) for p in range(3)], axis=1
    )
    piece = mm_nt(rows + anchor, parent_inv[...]).astype(BF16)
    prow[c] = piece

    def gather_rows(k):
        return remote(prow.at[c], prow.at[c], g1s.at[k], g1r.at[c], col=k)

    def gather_rows_from(k):
        return remote(prow.at[c], prow.at[k], g1s.at[k], g1r.at[k], col=k)

    def gather_cols(k):
        return remote(prow.at[c], pcol.at[c % 8], g2s.at[k], g2r.at[c % 8], row=k, col=cols_to)

    def gather_cols_from(k):
        return remote(
            prow.at[c], pcol.at[k], g2s.at[k], g2r.at[k], row=cols_from_row, col=cols_from_col + k
        )

    def is_other(k):
        return jnp.logical_not((k == r) & (cols_to == c))

    @pl.when(sends_cols)
    def _():
        def go(j):
            k = lax.rem(r + j, ROWS)

            @pl.when(is_other(k))
            def _():
                gather_cols(k).start()

            @pl.when(jnp.logical_not(is_other(k)))
            def _():
                pcol[c % 8] = piece

        each(1, 17, go)

    each(1, 16, lambda j: gather_rows(lax.rem(c + j, COLS)).start())

    def fourth(k):
        return remote(y.at[pl.ds(4 * k, 4)], z4.at[c], z4s.at[k], z4r.at[c], col=k)

    def fourth_from(k):
        return remote(y.at[pl.ds(4 * k, 4)], z4.at[k], z4s.at[k], z4r.at[k], col=k)

    def both(k, q):
        return (strip(64 * s + 4 * k + q).astype(F32) + xr[4 * k + q].astype(F32)).astype(BF16)

    def send_fourth(j):
        k = lax.rem(c + j, COLS)
        half(k).wait_recv()
        for q in range(4):
            y[4 * k + q] = both(k, q)
        fourth(k).start()

    each(1, 16, send_fourth)
    half(c).wait_recv()
    for q in range(4):
        z4[c, q] = both(c, q)

    def cols_rest(k):
        @pl.when(jnp.logical_not((cols_from_row == r) & (cols_from_col + k == c)))
        def _():
            gather_cols_from(k).wait_recv()

    each(0, 8, cols_rest)
    for chunk in range(4):
        def rows_rest(k):
            @pl.when(k != c)
            def _():
                gather_rows_from(k).wait_recv()
                fourth_from(k).wait_recv()

        each(4 * chunk, 4 * chunk + 4, rows_rest)
        left = prow[4 * chunk:4 * chunk + 4].reshape(256, 384)
        panel_ref[256 * chunk:256 * (chunk + 1), :] = left
        row_ids = 1024 * r + 256 * chunk + lax.broadcasted_iota(jnp.int32, (256, 128), 0)
        for q in range(4):
            right = pcol[2 * q:2 * q + 2].reshape(128, 384)
            front = z4[4 * chunk:4 * chunk + 4, q].astype(F32).reshape(256, 128)
            value = front - dot_nt(left, right)
            col_ids = 512 * (16 * s + c) + 128 * q + lax.broadcasted_iota(jnp.int32, (256, 128), 1)
            value = jnp.where((row_ids >= 384) & (col_ids >= 384), value, 0.0)
            update_ref[256 * chunk:256 * (chunk + 1), 128 * q:128 * (q + 1)] = value.astype(BF16)

    @pl.when(at_root)
    def _():
        each(1, 8, lambda k: corner_a(k).wait_send())

    @pl.when(holds & (c == 0))
    def _():
        each(1, 16, lambda k: corner_b(k).wait_send())

    @pl.when(holds)
    def _():
        each(1, 16, lambda j: corner_c(lax.rem(r + j, ROWS)).wait_send())

    @pl.when(sends_cols)
    def _():
        def gone(k):
            @pl.when(is_other(k))
            def _():
                gather_cols(k).wait_send()

        each(0, 16, gone)

    def all_gone(j):
        k = lax.rem(r + j, ROWS)
        first(k).wait_send()
        second(k).wait_send()
        k = lax.rem(c + j, COLS)
        third(k).wait_send()
        fourth(k).wait_send()
        gather_rows(k).wait_send()

    each(1, 16, all_gone)
    each(0, 16, lambda k: half(k).wait_send())
    swap.wait_send()
    swap_pivots.wait_send()


def front_step(maps, trailing, border, cross, inverse, pivot):
    vmem = pl.BlockSpec(memory_space=pltpu.VMEM)
    dma = pltpu.SemaphoreType.DMA
    buffers = [
        (768, 384), (768, 384),
        (6, 6, 8, 16, 128),
        (3, 97, 16, 128),
        (3, 128, 16, 128),
        (6, 8, 8, 16, 128),
        (97, 4, 16, 128),
        (64, 4, 16, 128), (64, 4, 16, 128),
        (3, 4, 16, 128), (3, 4, 16, 128),
        (64, 4, 16, 128),
        (16, 4, 4, 16, 128),
        (16, 64, 384), (8, 64, 384),
        (2, 3, 3, 8, 16, 128),
    ]
    counts = [16] * 12 + [8, 1, 16, 1, 16, 8, 2, 2, 16, 16, 4]
    return pl.pallas_call(
        front_kernel,
        out_shape=(
            jax.ShapeDtypeStruct((1024, 384), BF16),
            jax.ShapeDtypeStruct((1024, 512), BF16),
        ),
        in_specs=[pl.BlockSpec(memory_space=pltpu.SMEM)] + [vmem] * 5,
        out_specs=(vmem, vmem),
        scratch_shapes=[pltpu.VMEM(shape, BF16) for shape in buffers]
        + [pltpu.VMEM((384, 384), F32)]
        + FACTOR_SCRATCH
        + [dma((count,)) for count in counts],
        compiler_params=pltpu.CompilerParams(
            collective_id=0, has_side_effects=True, vmem_limit_bytes=50 << 20
        ),
        cost_estimate=pl.CostEstimate(flops=10**10, bytes_accessed=10**8, transcendentals=0),
    )(maps, trailing, border, cross, inverse, pivot)


def inverse_maps(child_maps):
    matches = child_maps[:, :, None] == jnp.arange(128, dtype=jnp.int32)
    source = jnp.arange(96, dtype=jnp.int32)[None, :, None]
    return jnp.min(jnp.where(matches, source, 96), axis=1).astype(jnp.int32)


def shards(child_pivot, child_border, child_trailing, parent_pivot, child_maps):
    across = [(16 * i + j, 16 * j + i) for i in range(ROWS) for j in range(COLS)]
    cross = lax.ppermute(child_border[0], ("row", "col"), across)
    inverse = child_inverse(child_pivot[0])
    return front_step(
        inverse_maps(child_maps), child_trailing[0], child_border[0], cross, inverse, parent_pivot
    )


def solution(mesh):
    placed = (P("sib", None, None), P("sib", "row", None), P("sib", "row", "col"), P(), P())
    return jax.shard_map(
        shards,
        mesh=mesh,
        in_specs=placed,
        out_specs=(P("row", None), P("row", ("sib", "col"))),
        check_vma=False,
    )
```

time: 796 us -> 297 us (0.37)
  the two profiles are of different devices: /device:TPU:4 before, /device:TPU:42 now
where the time goes in v1:
time: 297 us; the launch traced here: 296 us
  Pallas kernels  243 us (82%)
  waiting for transfers between devices  42 us (14%)
  starting transfers between devices  6.88 us (2%)
    pallas_call x1, Pallas kernels, front_step(): pl.pallas_call(front_kernel, out_shape=(jax.ShapeDtypeStruct((1024, 384),...  227 us
    ppermute x1, waiting for transfers between devices, shards(): cross = lax.ppermute(child_border[0], ('row', 'col'), across)  42 us
    pallas_call x1, Pallas kernels, child_inverse(): pl.pallas_call(child_kernel, out_shape=jax.ShapeDtypeStruct((384, 384), F...  15.7 us
    ppermute x1, starting transfers between devices, shards(): cross = lax.ppermute(child_border[0], ('row', 'col'), across)  6.88 us
  transfers between devices with their start and end apart: 1, of which 1 were waited for; matrix products, arithmetic and copies ran while one was open for 0% of the time, Pallas kernels for 5%

profile of v1, /device:TPU:42, one launch (start us, length us, event | category | flops | bytes accessed | tf_op | source)
XLA Modules:
  0.0 296.3 jit_solution(14924226975692942101)
XLA Ops:
  0.6 6.9 %collective-permute-start = (bf16[768,384]{1,0:T(8,128)(2,1)}, bf16[768,384]{1,0:T(8,128)(2,1)S(1)}, u32[]{:S(2)}, u32[]{:S(2)}) collective-permute-start(bf16[768,384]{1,0:T(8,128)(2,1)} %bitcast.3), channel_id=1, source_target_pairs={{0,0},{1,16},{2,32},{3,48},{4,64},{5,80},{6,96},{7,112},{8,128},{9... | collective-permute-start | bytes 1769480 | tf_op jit(solution)/shard_map/ppermute | solution.py:534
  7.5 0.8 select_reduce_fusion.maps_ref
  8.3 0.0 copy-start.1
  8.3 1.0 copy-done.1
  9.3 0.0 copy-start
  9.3 0.0 copy-start.2
  9.3 15.7 %shard_map.68.inverse_ref = f32[384,384]{1,0:T(8,128)S(1)} custom-call(bf16[384,384]{1,0:T(8,128)(2,1)S(1)} %bitcast.5), custom_call_target="tpu_custom_call" | custom-call | flops 2000000000 | bytes 1000000 | tf_op jit(solution)/shard_map/pallas_call | solution.py:142
  25.0 42.0 %collective-permute-done.cross_ref = bf16[768,384]{1,0:T(8,128)(2,1)S(1)} collective-permute-done((bf16[768,384]{1,0:T(8,128)(2,1)}, bf16[768,384]{1,0:T(8,128)(2,1)S(1)}, u32[]{:S(2)}, u32[]{:S(2)}) %collective-permute-start) | collective-permute-done | bytes 589856 | tf_op jit(solution)/shard_map/ppermute | solution.py:534
  67.0 0.0 copy-done
  67.0 0.0 copy-done.2
  67.0 227.4 %shard_map.69 = (bf16[1024,384]{1,0:T(8,128)(2,1)S(1)}, bf16[1024,512]{1,0:T(8,128)(2,1)S(1)}) custom-call(s32[2,128]{1,0:T(2,128)S(1)} %select_reduce_fusion.maps_ref, bf16[768,768]{1,0:T(8,128)(2,1)} %bitcast.6, bf16[768,384]{1,0:T(8,128)(2,1)S(1)} %bitcast.4, bf16[768,384]{1,0:T(8,128)(2,1)S(1)} %collective-permute-done.cross_ref, ...), custom_call_target="tpu_custom_call" | custom-call | flops 10000000000 | bytes 100000000 | tf_op jit(solution)/shard_map/pallas_call | solution.py:507
  294.4 0.9 copy.9
  295.3 1.0 copy.10
Async XLA Ops:
  0.6 66.3 %collective-permute-start = (bf16[768,384]{1,0:T(8,128)(2,1)}, bf16[768,384]{1,0:T(8,128)(2,1)S(1)}, u32[]{:S(2)}, u32[]{:S(2)}) collective-permute-start(bf16[768,384]{1,0:T(8,128)(2,1)} %bitcast.3), channel_id=1, source_target_pairs={{0,0},{1,16},{2,32},{3,48},{4,64},{5,80},{6,96},{7,112},{8,128},{9... | collective-permute-start | bytes 1769480 | tf_op jit(solution)/shard_map/ppermute | solution.py:534
  8.3 1.0 copy-start.1
  9.3 57.7 %copy-start = (bf16[1,768,384]{2,1,0:T(8,128)(2,1)S(1)}, bf16[1,768,384]{2,1,0:T(8,128)(2,1)}, u32[]{:S(2)}) copy-start(bf16[1,768,384]{2,1,0:T(8,128)(2,1)} %param.6) | copy-start | bytes 1769476
  9.3 57.7 %copy-start.2 = (bf16[384,384]{1,0:T(8,128)(2,1)S(1)}, bf16[384,384]{1,0:T(8,128)(2,1)}, u32[]{:S(2)}) copy-start(bf16[384,384]{1,0:T(8,128)(2,1)} %pivot_ref.1) | copy-start | bytes 884740

commit v2 on v1

--- a/solution.py
+++ b/solution.py
@@ -75,7 +75,7 @@
             m = m - w[0] * m1p - w[1] * m2p - u3 * m3p - u4 * m4p
 
 
-def factor_inverse(a_ref, out_ref, s_ref, i_ref, l_ref):
+def factor_inverse(a_ref, out_ref, s_ref, i_ref, l_ref, between=None):
     n = 384
     a = a_ref[...]
     rows = lax.broadcasted_iota(jnp.int32, (n, n), 0)
@@ -102,6 +102,8 @@
             a_ref[b[2], b[2]] = a_ref[b[2], b[2]] - mm_nt(l31, l31)
             l_ref[0] = mm(l21, inv)
             l_ref[1] = mm(l31, inv)
+            if between is not None:
+                between()
 
         @pl.when(k == 1)
         def _():
@@ -133,23 +135,6 @@
 ]
 
 
-def child_kernel(pivot_ref, out_ref, a_ref, s_ref, i_ref, l_ref):
-    a_ref[...] = pivot_ref[...].astype(F32)
-    factor_inverse(a_ref, out_ref, s_ref, i_ref, l_ref)
-
-
-def child_inverse(pivot):
-    return pl.pallas_call(
-        child_kernel,
-        out_shape=jax.ShapeDtypeStruct((384, 384), F32),
-        in_specs=[pl.BlockSpec(memory_space=pltpu.VMEM)],
-        out_specs=pl.BlockSpec(memory_space=pltpu.VMEM),
-        scratch_shapes=FACTOR_SCRATCH,
-        compiler_params=pltpu.CompilerParams(vmem_limit_bytes=32 << 20),
-        cost_estimate=pl.CostEstimate(flops=2 * 10**9, bytes_accessed=10**6, transcendentals=0),
-    )(pivot)
-
-
 def panel_of(border, inverse):
     high = inverse.astype(BF16)
     rest = inverse - high.astype(F32)
@@ -159,12 +144,12 @@
 
 
 def front_kernel(
-    maps_ref, trailing_ref, border_ref, cross_ref, inverse_ref, pivot_ref,
+    maps_ref, trailing_ref, border_ref, child_ref, pivot_ref,
     panel_ref, update_ref,
-    pr, pc, u, z1, w1, v, z3, xs, xr, fs, fr, y, z4, prow, pcol, crn, parent_inv,
+    bx, pr, pc, u, z1, w1, v, z3, xs, xr, fs, fr, y, z4, prow, pcol, crn, parent_inv,
     a_ref, s_ref, i_ref, l_ref,
-    z1s, z1r, z2s, z2r, z3s, z3r, z4s, z4r, g1s, g1r, g2s, g2r,
-    cas, car, cbs, cbr, ccs, ccr, sws, swr, xss, xsr, lsem,
+    b1s, b1r, b2s, b2r, z1s, z1r, z2s, z2r, z3s, z3r, z4s, z4r, g1s, g1r, g2s, g2r,
+    cas, car, cbs, cbr, ccs, ccr, sws, swr, xss, xsr, hs, hr, lsem,
 ):
     s = lax.axis_index("sib")
     r = lax.axis_index("row")
@@ -206,18 +191,64 @@
 
     each(0, 8, greet_cols)
 
-    inverse = inverse_ref[...]
-    pr[...] = panel_of(border_ref[...], inverse)
-    pc[...] = panel_of(cross_ref[...], inverse)
+    expected = 31 + jnp.where(sends_cols, 16 - (cols_to == c).astype(jnp.int32), 0)
+    pl.semaphore_wait(barrier, expected)
+
+    is_root = r == c
+
+    def scatter(k):
+        return remote(border_ref.at[k], bx.at[k], b1s.at[k], b1r.at[0], row=k)
+
+    def scatter_here():
+        return remote(border_ref.at[r], bx.at[r], b1s.at[r], b1r.at[0], row=c)
+
+    def spread(k):
+        return remote(bx.at[r], bx.at[r], b2s.at[k], b2r.at[r], row=k)
+
+    def spread_from(k):
+        return remote(bx.at[r], bx.at[k], b2s.at[k], b2r.at[k], row=k)
+
+    def to_others(body):
+        def go(j):
+            k = lax.rem(r + j, ROWS)
+
+            @pl.when(k != c)
+            def _():
+                body(k)
+
+        each(1, 16, go)
+
+    own_border = pltpu.make_async_copy(border_ref, bx, lsem.at[4])
+
+    @pl.when(is_root)
+    def _():
+        each(1, 16, lambda j: scatter(lax.rem(r + j, ROWS)).start())
+        own_border.start()
+        own_border.wait()
+
+    def spread_border():
+        @pl.when(jnp.logical_not(is_root))
+        def _():
+            scatter_here().wait_recv()
+
+        to_others(lambda k: spread(k).start())
+
+    a_ref[...] = child_ref[...].astype(F32)
+    factor_inverse(a_ref, parent_inv, s_ref, i_ref, l_ref, spread_border)
+    inverse = parent_inv[...]
+    pr[...] = panel_of(border_ref[...].reshape(768, 384), inverse)
+
+    @pl.when(jnp.logical_not(is_root))
+    def _():
+        each(1, 16, lambda j: spread_from(lax.rem(r + j, ROWS)).wait_recv())
+
+    pc[...] = panel_of(bx[...].reshape(768, 384), inverse)
     for i in range(6):
         rows = pl.ds(128 * i, 128)
         value = trailing_ref[rows, :].astype(F32) - dot_nt(pr[rows, :], pc[...])
         value = value.astype(BF16)
         for q in range(6):
             u[q, i] = value[:, 128 * q:128 * (q + 1)].reshape(8, 16, 128)
-
-    expected = 31 + jnp.where(sends_cols, 16 - (cols_to == c).astype(jnp.int32), 0)
-    pl.semaphore_wait(barrier, expected)
 
     at_root = (r == 0) & (c == 0)
     holds = r < 8
@@ -370,11 +401,20 @@
     piece = mm_nt(rows + anchor, parent_inv[...]).astype(BF16)
     prow[c] = piece
 
+    mine = pl.ds(pl.multiple_of(32 * s, 32), 32)
+    theirs = pl.ds(pl.multiple_of(32 * other, 32), 32)
+
     def gather_rows(k):
-        return remote(prow.at[c], prow.at[c], g1s.at[k], g1r.at[c], col=k)
+        return remote(prow.at[c, mine], prow.at[c, mine], g1s.at[k], g1r.at[c], col=k)
 
     def gather_rows_from(k):
-        return remote(prow.at[c], prow.at[k], g1s.at[k], g1r.at[k], col=k)
+        return remote(prow.at[c, mine], prow.at[k, mine], g1s.at[k], g1r.at[k], col=k)
+
+    def hand_rows(k):
+        return remote(prow.at[k, mine], prow.at[k, mine], hs.at[k], hr.at[k], sib=other)
+
+    def hand_rows_from(k):
+        return remote(prow.at[k, mine], prow.at[k, theirs], hs.at[k], hr.at[k], sib=other)
 
     def gather_cols(k):
         return remote(prow.at[c], pcol.at[c % 8], g2s.at[k], g2r.at[c % 8], row=k, col=cols_to)
@@ -431,11 +471,18 @@
             gather_cols_from(k).wait_recv()
 
     each(0, 8, cols_rest)
+
+    def hand(j):
+        k = lax.rem(c + COLS - j, COLS)
+        gather_rows_from(k).wait_recv()
+        hand_rows(k).start()
+
+    each(1, 16, hand)
     for chunk in range(4):
         def rows_rest(k):
             @pl.when(k != c)
             def _():
-                gather_rows_from(k).wait_recv()
+                hand_rows_from(k).wait_recv()
                 fourth_from(k).wait_recv()
 
         each(4 * chunk, 4 * chunk + 4, rows_rest)
@@ -450,6 +497,12 @@
             value = jnp.where((row_ids >= 384) & (col_ids >= 384), value, 0.0)
             update_ref[256 * chunk:256 * (chunk + 1), 128 * q:128 * (q + 1)] = value.astype(BF16)
 
+    @pl.when(is_root)
+    def _():
+        each(1, 16, lambda j: scatter(lax.rem(r + j, ROWS)).wait_send())
+
+    to_others(lambda k: spread(k).wait_send())
+
     @pl.when(at_root)
     def _():
         each(1, 8, lambda k: corner_a(k).wait_send())
@@ -479,6 +532,7 @@
         third(k).wait_send()
         fourth(k).wait_send()
         gather_rows(k).wait_send()
+        hand_rows(k).wait_send()
 
     each(1, 16, all_gone)
     each(0, 16, lambda k: half(k).wait_send())
@@ -486,10 +540,11 @@
     swap_pivots.wait_send()
 
 
-def front_step(maps, trailing, border, cross, inverse, pivot):
+def front_step(maps, trailing, border, child, pivot):
     vmem = pl.BlockSpec(memory_space=pltpu.VMEM)
     dma = pltpu.SemaphoreType.DMA
     buffers = [
+        (16, 48, 384),
         (768, 384), (768, 384),
         (6, 6, 8, 16, 128),
         (3, 97, 16, 128),
@@ -503,14 +558,14 @@
         (16, 64, 384), (8, 64, 384),
         (2, 3, 3, 8, 16, 128),
     ]
-    counts = [16] * 12 + [8, 1, 16, 1, 16, 8, 2, 2, 16, 16, 4]
+    counts = [16, 1] + [16] * 14 + [8, 1, 16, 1, 16, 8, 2, 2, 16, 16, 16, 16, 5]
     return pl.pallas_call(
         front_kernel,
         out_shape=(
             jax.ShapeDtypeStruct((1024, 384), BF16),
             jax.ShapeDtypeStruct((1024, 512), BF16),
         ),
-        in_specs=[pl.BlockSpec(memory_space=pltpu.SMEM)] + [vmem] * 5,
+        in_specs=[pl.BlockSpec(memory_space=pltpu.SMEM)] + [vmem] * 4,
         out_specs=(vmem, vmem),
         scratch_shapes=[pltpu.VMEM(shape, BF16) for shape in buffers]
         + [pltpu.VMEM((384, 384), F32)]
@@ -520,7 +575,7 @@
             collective_id=0, has_side_effects=True, vmem_limit_bytes=50 << 20
         ),
         cost_estimate=pl.CostEstimate(flops=10**10, bytes_accessed=10**8, transcendentals=0),
-    )(maps, trailing, border, cross, inverse, pivot)
+    )(maps, trailing, border, child, pivot)
 
 
 def inverse_maps(child_maps):
@@ -530,12 +585,8 @@
 
 
 def shards(child_pivot, child_border, child_trailing, parent_pivot, child_maps):
-    across = [(16 * i + j, 16 * j + i) for i in range(ROWS) for j in range(COLS)]
-    cross = lax.ppermute(child_border[0], ("row", "col"), across)
-    inverse = child_inverse(child_pivot[0])
-    return front_step(
-        inverse_maps(child_maps), child_trailing[0], child_border[0], cross, inverse, parent_pivot
-    )
+    border = child_border[0].reshape(16, 48, 384)
+    return front_step(inverse_maps(child_maps), child_trailing[0], border, child_pivot[0], parent_pivot)
 
 
 def solution(mesh):

time: 297 us -> 211 us (0.71)
  the two profiles are of different devices: /device:TPU:42 before, /device:TPU:2 now
where the time goes in v2:
time: 211 us; the launch traced here: 210 us
  Pallas kernels  204 us (97%)
  local copies, waits for them, and re-layouts  4.83 us (2%)
    pallas_call x1, Pallas kernels, front_step(): pl.pallas_call(front_kernel, out_shape=(jax.ShapeDtypeStruct((1024, 384),...  204 us
    unnamed x8, local copies, waits for them, and re-layouts  4.83 us

profile of v2, /device:TPU:2, one launch (start us, length us, event | category | flops | bytes accessed | tf_op | source)
XLA Modules:
  0.0 210.3 jit_solution(11122720752496902437)
XLA Ops:
  0.6 0.8 select_reduce_fusion.maps_ref
  1.4 0.0 copy-start
  1.4 1.1 copy-done
  2.5 0.0 copy-start.1
  2.5 1.0 copy-done.1
  3.4 0.0 copy-start.2
  3.4 1.0 copy-done.2
  4.4 204.0 %shard_map.68 = (bf16[1024,384]{1,0:T(8,128)(2,1)S(1)}, bf16[1024,512]{1,0:T(8,128)(2,1)S(1)}) custom-call(s32[2,128]{1,0:T(2,128)S(1)} %select_reduce_fusion.maps_ref, bf16[768,768]{1,0:T(8,128)(2,1)} %bitcast.5, bf16[16,48,384]{2,1,0:T(8,128)(2,1)S(1)} %bitcast.3, bf16[384,384]{1,0:T(8,128)(2,1)S(1)} %bitcast.4, bf16[384,384]{1,0:T(8,128)(2,1)S(1)} %copy-done.2), custom_call_target="tpu_custom_call" | custom-call | flops 10000000000 | bytes 100000000 | tf_op jit(solution)/shard_map/pallas_call | solution.py:562
  208.4 0.9 copy.9
  209.3 1.0 copy.10
Async XLA Ops:
  1.4 1.1 copy-start
  2.5 1.0 copy-start.1
  3.4 1.0 copy-start.2

commit v3 on v2

--- a/solution.py
+++ b/solution.py
@@ -146,10 +146,10 @@
 def front_kernel(
     maps_ref, trailing_ref, border_ref, child_ref, pivot_ref,
     panel_ref, update_ref,
-    bx, pr, pc, u, z1, w1, v, z3, xs, xr, fs, fr, y, z4, prow, pcol, crn, parent_inv,
+    bx, pr, pc, u, z1, w1, z3, zf, xs, xr, fs, fr, y, z4, prow, pcol, crn, parent_inv,
     a_ref, s_ref, i_ref, l_ref,
-    b1s, b1r, b2s, b2r, z1s, z1r, z2s, z2r, z3s, z3r, z4s, z4r, g1s, g1r, g2s, g2r,
-    cas, car, cbs, cbr, ccs, ccr, sws, swr, xss, xsr, hs, hr, lsem,
+    b1s, b1r, b2s, b2r, z1s, z1r, z2s, z2r, z4s, z4r, g1s, g1r, g2s, g2r,
+    cas, car, cbs, cbr, ccs, ccr, sws, swr, xss, xsr, hs, hr, lsem, told,
 ):
     s = lax.axis_index("sib")
     r = lax.axis_index("row")
@@ -182,17 +182,13 @@
     each(1, 16, greet)
     pl.semaphore_signal(barrier, inc=1, device_id={"sib": other}, device_id_type=MESH)
 
-    def greet_cols(k):
-        @pl.when(jnp.logical_not((cols_from_row == r) & (cols_from_col + k == c)))
-        def _():
-            pl.semaphore_signal(
-                barrier, inc=1, device_id={"row": cols_from_row, "col": cols_from_col + k}, device_id_type=MESH
-            )
-
-    each(0, 8, greet_cols)
-
-    expected = 31 + jnp.where(sends_cols, 16 - (cols_to == c).astype(jnp.int32), 0)
-    pl.semaphore_wait(barrier, expected)
+    pl.semaphore_wait(barrier, 31)
+
+    def greet_again(j):
+        pl.semaphore_signal(told, inc=1, device_id={"col": lax.rem(c + j, COLS)}, device_id_type=MESH)
+
+    each(1, 16, greet_again)
+    keeps = c % 2 == r // 8
 
     is_root = r == c
 
@@ -263,6 +259,15 @@
         own.start()
         own.wait()
 
+    def corner_b(k):
+        return remote(crn.at[s, :, :, r], crn.at[s, :, :, r], cbs.at[k], cbr.at[0], col=k)
+
+    def corner_c(k):
+        return remote(crn.at[s, :, :, r], crn.at[s, :, :, r], ccs.at[k], ccr.at[r], row=k)
+
+    def corner_c_from(k):
+        return remote(crn.at[s, :, :, k], crn.at[s, :, :, k], ccs.at[k], ccr.at[k], row=k)
+
     def first(k):
         return remote(
             u.at[pl.ds(3 * (k % 2), 3), :, k // 2], z1.at[:, pl.ds(6 * r, 6)], z1s.at[k], z1r.at[r], row=k
@@ -273,55 +278,21 @@
             u.at[pl.ds(3 * h, 3), :, g], z1.at[:, pl.ds(6 * k, 6)], z1s.at[k], z1r.at[k], row=k
         )
 
-    each(1, 16, lambda j: first(lax.rem(r + j, ROWS)).start())
+    each(1, 4, lambda j: first(lax.rem(r + j, ROWS)).start())
     own1 = pltpu.make_async_copy(u.at[pl.ds(3 * h, 3), :, g], z1.at[:, pl.ds(6 * r, 6)], lsem.at[1])
     own1.start()
+
+    @pl.when(holds & (c == 0))
+    def _():
+        @pl.when(r > 0)
+        def _():
+            corner_a(r).wait_recv()
+        each(1, 16, lambda k: corner_b(k).start())
+
+    each(4, 9, lambda j: first(lax.rem(r + j, ROWS)).start())
     z1[:, 96] = jnp.zeros((3, 16, 128), BF16)
     z3[96] = jnp.zeros((4, 16, 128), BF16)
-    own1.wait()
-
-    def corner_b(k):
-        return remote(crn.at[s, :, :, r], crn.at[s, :, :, r], cbs.at[k], cbr.at[0], col=k)
-
-    @pl.when(holds & (c == 0))
-    def _():
-        @pl.when(r > 0)
-        def _():
-            corner_a(r).wait_recv()
-        each(1, 16, lambda k: corner_b(k).start())
-
-    each(1, 16, lambda j: first_from(lax.rem(r + j, ROWS)).wait_recv())
-
-    def second(k):
-        return remote(
-            w1.at[:, pl.ds(8 * k, 8)], v.at[pl.ds(3 * h, 3), :, g], z2s.at[k], z2r.at[r], row=k
-        )
-
-    def second_from(k):
-        return remote(
-            w1.at[:, pl.ds(8 * r, 8)], v.at[pl.ds(3 * (k % 2), 3), :, k // 2], z2s.at[k], z2r.at[k], row=k
-        )
-
-    def widen_rows(k):
-        for j in range(8):
-            p = 8 * k + j
-            w1[:, p] = z1[:, maps_ref[s, p]]
-
-    def send_second(j):
-        k = lax.rem(r + j, ROWS)
-        widen_rows(k)
-        second(k).start()
-
-    each(1, 16, send_second)
-    widen_rows(r)
-    own2 = pltpu.make_async_copy(w1.at[:, pl.ds(8 * r, 8)], v.at[pl.ds(3 * h, 3), :, g], lsem.at[2])
-    own2.start()
-
-    def corner_c(k):
-        return remote(crn.at[s, :, :, r], crn.at[s, :, :, r], ccs.at[k], ccr.at[r], row=k)
-
-    def corner_c_from(k):
-        return remote(crn.at[s, :, :, k], crn.at[s, :, :, k], ccs.at[k], ccr.at[k], row=k)
+    zf[3] = jnp.zeros((4, 16, 128), BF16)
 
     @pl.when(holds)
     def _():
@@ -330,23 +301,7 @@
             corner_b(c).wait_recv()
         each(1, 16, lambda j: corner_c(lax.rem(r + j, ROWS)).start())
 
-    own2.wait()
-    each(1, 16, lambda j: second_from(lax.rem(r + j, ROWS)).wait_recv())
-
-    def third(k):
-        return remote(
-            v.at[:, k // 2, pl.ds(4 * (k % 2), 4)], z3.at[pl.ds(6 * c, 6)], z3s.at[k], z3r.at[c], col=k
-        )
-
-    def third_from(k):
-        return remote(
-            v.at[:, c // 2, pl.ds(4 * (c % 2), 4)], z3.at[pl.ds(6 * k, 6)], z3s.at[k], z3r.at[k], col=k
-        )
-    each(1, 16, lambda j: third(lax.rem(c + j, COLS)).start())
-    own3 = pltpu.make_async_copy(
-        v.at[:, c // 2, pl.ds(4 * (c % 2), 4)], z3.at[pl.ds(6 * c, 6)], lsem.at[3]
-    )
-    own3.start()
+    each(9, 16, lambda j: first(lax.rem(r + j, ROWS)).start())
 
     def corner_rest(k):
         @pl.when(k != r)
@@ -357,6 +312,47 @@
     swap = remote(crn.at[s], crn.at[s], sws.at[0], swr.at[0], sib=other)
     swap_back = remote(crn.at[s], crn.at[other], sws.at[0], swr.at[0], sib=other)
     swap.start()
+    own1.wait()
+    each(1, 16, lambda j: first_from(lax.rem(r + j, ROWS)).wait_recv())
+    pl.semaphore_wait(told, 15)
+
+    def second(k, l):
+        return remote(
+            w1.at[:, 8 * k + l // 2], z3.at[pl.ds(6 * c + 3 * h, 3), g % 4],
+            z2s.at[8 * k + l // 2], z2r.at[8 * c + r % 8], row=k, col=l
+        )
+
+    def second_from(k, l):
+        return remote(
+            w1.at[:, 8 * r + c // 2], z3.at[pl.ds(6 * l + 3 * (k % 2), 3), k // 2 % 4],
+            z2s.at[8 * r + c // 2], z2r.at[8 * l + k % 8], row=k, col=l
+        )
+
+    def here2():
+        return pltpu.make_async_copy(
+            w1.at[:, 8 * r + c // 2], z3.at[pl.ds(6 * c + 3 * h, 3), g % 4], lsem.at[2]
+        )
+
+    def send_second(j):
+        k = lax.rem(r + j, ROWS)
+
+        def go(i):
+            l = lax.rem(2 * i + c, COLS) // 2 * 2 + r // 8
+            p = 8 * k + l // 2
+            w1[:, p] = z1[:, maps_ref[s, p]]
+
+            @pl.when((k == r) & (l == c))
+            def _():
+                here2().start()
+
+            @pl.when(jnp.logical_not((k == r) & (l == c)))
+            def _():
+                second(k, l).start()
+
+        each(0, 8, go)
+
+    each(1, 17, send_second)
+
     swap_back.wait_recv()
     for p in range(3):
         for q in range(3):
@@ -369,28 +365,27 @@
             a_ref[128 * p:128 * (p + 1), 128 * q:128 * (q + 1)] = total
     factor_inverse(a_ref, parent_inv, s_ref, i_ref, l_ref)
 
-    own3.wait()
-    each(1, 16, lambda j: third_from(lax.rem(c + j, COLS)).wait_recv())
-
-    def strip(p):
-        return z3[maps_ref[s, p]]
-
+    @pl.when(keeps)
+    def _():
+        here2().wait()
+
+    def not_self(k, l):
+        return jnp.logical_not((k == r) & (l == c))
+
+    def pivots_rest(j):
+        k = 8 * (c % 2) + 2 * j
+
+        @pl.when(not_self(k, 0))
+        def _():
+            second_from(k, 0).wait_recv()
+
+    each(0, 4, pivots_rest)
     for p in range(3):
-        fs[p] = strip(p)
+        zf[p] = z3[p]
+    for p in range(3):
+        fs[p] = zf[jnp.minimum(maps_ref[s, p], 3)]
     swap_pivots = remote(fs, fr, sws.at[1], swr.at[1], sib=other)
     swap_pivots.start()
-
-    def half(k):
-        return remote(xs.at[pl.ds(4 * k, 4)], xr.at[pl.ds(4 * k, 4)], xss.at[k], xsr.at[k], sib=other)
-
-    def send_half(j):
-        k = lax.rem(c + j, COLS)
-        for q in range(4):
-            xs[4 * k + q] = strip(64 * other + 4 * k + q)
-        half(k).start()
-
-    each(1, 17, send_half)
-
     swap_pivots.wait_recv()
     first_rows = (r == 0) & (c < 6)
     start_row = pl.multiple_of(64 * jnp.minimum(c, 5), 64)
@@ -443,6 +438,29 @@
         each(1, 17, go)
 
     each(1, 16, lambda j: gather_rows(lax.rem(c + j, COLS)).start())
+
+    def second_rest(j):
+        k, l = 8 * (c % 2) + j % 8, j // 8
+
+        @pl.when(not_self(k, l) & ((l > 0) | (k % 2 == 1)))
+        def _():
+            second_from(k, l).wait_recv()
+
+    each(0, 128, second_rest)
+
+    def strip(p):
+        return z3[maps_ref[s, p]]
+
+    def half(k):
+        return remote(xs.at[pl.ds(4 * k, 4)], xr.at[pl.ds(4 * k, 4)], xss.at[k], xsr.at[k], sib=other)
+
+    def send_half(j):
+        k = lax.rem(c + j, COLS)
+        for q in range(4):
+            xs[4 * k + q] = strip(64 * other + 4 * k + q)
+        half(k).start()
+
+    each(1, 17, send_half)
 
     def fourth(k):
         return remote(y.at[pl.ds(4 * k, 4)], z4.at[c], z4s.at[k], z4r.at[c], col=k)
@@ -527,14 +545,21 @@
     def all_gone(j):
         k = lax.rem(r + j, ROWS)
         first(k).wait_send()
-        second(k).wait_send()
         k = lax.rem(c + j, COLS)
-        third(k).wait_send()
         fourth(k).wait_send()
         gather_rows(k).wait_send()
         hand_rows(k).wait_send()
 
     each(1, 16, all_gone)
+
+    def second_gone(j):
+        k, l = j // 8, 2 * (j % 8) + r // 8
+
+        @pl.when(jnp.logical_not((k == r) & (l == c)))
+        def _():
+            second(k, l).wait_send()
+
+    each(0, 128, second_gone)
     each(0, 16, lambda k: half(k).wait_send())
     swap.wait_send()
     swap_pivots.wait_send()
@@ -549,8 +574,8 @@
         (6, 6, 8, 16, 128),
         (3, 97, 16, 128),
         (3, 128, 16, 128),
-        (6, 8, 8, 16, 128),
         (97, 4, 16, 128),
+        (4, 4, 16, 128),
         (64, 4, 16, 128), (64, 4, 16, 128),
         (3, 4, 16, 128), (3, 4, 16, 128),
         (64, 4, 16, 128),
@@ -558,7 +583,7 @@
         (16, 64, 384), (8, 64, 384),
         (2, 3, 3, 8, 16, 128),
     ]
-    counts = [16, 1] + [16] * 14 + [8, 1, 16, 1, 16, 8, 2, 2, 16, 16, 16, 16, 5]
+    counts = [16, 1] + [16] * 4 + [128] * 2 + [16] * 6 + [8, 1, 16, 1, 16, 8, 2, 2, 16, 16, 16, 16, 5]
     return pl.pallas_call(
         front_kernel,
         out_shape=(
@@ -570,7 +595,8 @@
         scratch_shapes=[pltpu.VMEM(shape, BF16) for shape in buffers]
         + [pltpu.VMEM((384, 384), F32)]
         + FACTOR_SCRATCH
-        + [dma((count,)) for count in counts],
+        + [dma((count,)) for count in counts]
+        + [pltpu.SemaphoreType.REGULAR],
         compiler_params=pltpu.CompilerParams(
             collective_id=0, has_side_effects=True, vmem_limit_bytes=50 << 20
         ),

time: 211 us -> 178 us (0.84)
  the two profiles are of different devices: /device:TPU:2 before, /device:TPU:7 now
where the time goes in v3:
time: 178 us; the launch traced here: 176 us
  Pallas kernels  170 us (96%)
  local copies, waits for them, and re-layouts  4.83 us (3%)
    pallas_call x1, Pallas kernels, front_step(): pl.pallas_call(front_kernel, out_shape=(jax.ShapeDtypeStruct((1024, 384),...  170 us
    unnamed x8, local copies, waits for them, and re-layouts  4.83 us

profile of v3, /device:TPU:7, one launch (start us, length us, event | category | flops | bytes accessed | tf_op | source)
XLA Modules:
  0.0 176.5 jit_solution(17383247888004278640)
XLA Ops:
  0.6 0.8 select_reduce_fusion.maps_ref
  1.4 0.0 copy-start
  1.4 1.1 copy-done
  2.5 0.0 copy-start.1
  2.5 1.0 copy-done.1
  3.4 0.0 copy-start.2
  3.4 1.0 copy-done.2
  4.4 170.2 %shard_map.68 = (bf16[1024,384]{1,0:T(8,128)(2,1)S(1)}, bf16[1024,512]{1,0:T(8,128)(2,1)S(1)}) custom-call(s32[2,128]{1,0:T(2,128)S(1)} %select_reduce_fusion.maps_ref, bf16[768,768]{1,0:T(8,128)(2,1)} %bitcast.5, bf16[16,48,384]{2,1,0:T(8,128)(2,1)S(1)} %bitcast.3, bf16[384,384]{1,0:T(8,128)(2,1)S(1)} %bitcast.4, bf16[384,384]{1,0:T(8,128)(2,1)S(1)} %copy-done.2), custom_call_target="tpu_custom_call" | custom-call | flops 10000000000 | bytes 100000000 | tf_op jit(solution)/shard_map/pallas_call | solution.py:587
  174.6 0.9 copy.9
  175.5 1.0 copy.10
Async XLA Ops:
  1.4 1.1 copy-start
  2.5 1.0 copy-start.1
  3.4 1.0 copy-start.2

commit v4 on v3

--- a/solution.py
+++ b/solution.py
@@ -146,7 +146,7 @@
 def front_kernel(
     maps_ref, trailing_ref, border_ref, child_ref, pivot_ref,
     panel_ref, update_ref,
-    bx, pr, pc, u, z1, w1, z3, zf, xs, xr, fs, fr, y, z4, prow, pcol, crn, parent_inv,
+    bx, pr, pc, u, cu, z1, w1, z3, zf, xs, xr, fs, fr, y, z4, prow, pcol, crn, parent_inv,
     a_ref, s_ref, i_ref, l_ref,
     b1s, b1r, b2s, b2r, z1s, z1r, z2s, z2r, z4s, z4r, g1s, g1r, g2s, g2r,
     cas, car, cbs, cbr, ccs, ccr, sws, swr, xss, xsr, hs, hr, lsem, told,
@@ -244,29 +244,32 @@
         value = trailing_ref[rows, :].astype(F32) - dot_nt(pr[rows, :], pc[...])
         value = value.astype(BF16)
         for q in range(6):
-            u[q, i] = value[:, 128 * q:128 * (q + 1)].reshape(8, 16, 128)
+            tile = value[:, 128 * q:128 * (q + 1)].reshape(8, 16, 128)
+            u[q, i] = tile
+            if q <= i < 3:
+                cu[:, i * (i + 1) // 2 + q] = tile
 
     at_root = (r == 0) & (c == 0)
     holds = r < 8
 
     def corner_a(k):
-        return remote(u.at[0:3, 0:3, k], crn.at[s, :, :, k], cas.at[k], car.at[0], row=k)
+        return remote(cu.at[k], crn.at[s, k], cas.at[k], car.at[0], row=k)
 
     @pl.when(at_root)
     def _():
         each(1, 8, lambda k: corner_a(k).start())
-        own = pltpu.make_async_copy(u.at[0:3, 0:3, 0], crn.at[s, :, :, 0], lsem.at[0])
+        own = pltpu.make_async_copy(cu.at[0], crn.at[s, 0], lsem.at[0])
         own.start()
         own.wait()
 
     def corner_b(k):
-        return remote(crn.at[s, :, :, r], crn.at[s, :, :, r], cbs.at[k], cbr.at[0], col=k)
+        return remote(crn.at[s, r], crn.at[s, r], cbs.at[k], cbr.at[0], col=k)
 
     def corner_c(k):
-        return remote(crn.at[s, :, :, r], crn.at[s, :, :, r], ccs.at[k], ccr.at[r], row=k)
+        return remote(crn.at[s, r], crn.at[s, r], ccs.at[k], ccr.at[r], row=k)
 
     def corner_c_from(k):
-        return remote(crn.at[s, :, :, k], crn.at[s, :, :, k], ccs.at[k], ccr.at[k], row=k)
+        return remote(crn.at[s, k], crn.at[s, k], ccs.at[k], ccr.at[k], row=k)
 
     def first(k):
         return remote(
@@ -355,12 +358,13 @@
 
     swap_back.wait_recv()
     for p in range(3):
-        for q in range(3):
+        for q in range(p + 1):
             total = pivot_ref[128 * p:128 * (p + 1), 128 * q:128 * (q + 1)].astype(F32)
             for child in range(2):
                 i, j = maps_ref[child, p], maps_ref[child, q]
                 present = (i < 3) & (j < 3)
-                block = crn[child, jnp.minimum(j, 2), jnp.minimum(i, 2)].astype(F32).reshape(128, 128)
+                i, j = jnp.minimum(i, 2), jnp.minimum(j, 2)
+                block = crn[child, :, i * (i + 1) // 2 + j].astype(F32).reshape(128, 128)
                 total = total + jnp.where(present, block, 0.0)
             a_ref[128 * p:128 * (p + 1), 128 * q:128 * (q + 1)] = total
     factor_inverse(a_ref, parent_inv, s_ref, i_ref, l_ref)
@@ -572,6 +576,7 @@
         (16, 48, 384),
         (768, 384), (768, 384),
         (6, 6, 8, 16, 128),
+        (8, 6, 16, 128),
         (3, 97, 16, 128),
         (3, 128, 16, 128),
         (97, 4, 16, 128),
@@ -581,7 +586,7 @@
         (64, 4, 16, 128),
         (16, 4, 4, 16, 128),
         (16, 64, 384), (8, 64, 384),
-        (2, 3, 3, 8, 16, 128),
+        (2, 8, 6, 16, 128),
     ]
     counts = [16, 1] + [16] * 4 + [128] * 2 + [16] * 6 + [8, 1, 16, 1, 16, 8, 2, 2, 16, 16, 16, 16, 5]
     return pl.pallas_call(

time: 178 us -> 174 us (0.978)
  Pallas kernels: 170 us -> 168 us
    pallas_call x1, Pallas kernels: 170 us -> 168 us  [front_step(): pl.pallas_call(front_kernel, out_shape=(jax.ShapeDtypeStruct((1024, 384),...]
where the time goes in v4:
time: 174 us
  Pallas kernels  168 us (97%)
  local copies, waits for them, and re-layouts  4.83 us (3%)
    pallas_call x1, Pallas kernels, front_step(): pl.pallas_call(front_kernel, out_shape=(jax.ShapeDtypeStruct((1024, 384),...  168 us
    unnamed x8, local copies, waits for them, and re-layouts  4.83 us

profile of v4, /device:TPU:7, one launch (start us, length us, event | category | flops | bytes accessed | tf_op | source)
XLA Modules:
  0.0 174.0 jit_solution(2131452357394150693)
XLA Ops:
  0.6 0.8 select_reduce_fusion.maps_ref
  1.4 0.0 copy-start
  1.4 1.1 copy-done
  2.5 0.0 copy-start.1
  2.5 1.0 copy-done.1
  3.4 0.0 copy-start.2
  3.4 1.0 copy-done.2
  4.4 167.7 %shard_map.68 = (bf16[1024,384]{1,0:T(8,128)(2,1)S(1)}, bf16[1024,512]{1,0:T(8,128)(2,1)S(1)}) custom-call(s32[2,128]{1,0:T(2,128)S(1)} %select_reduce_fusion.maps_ref, bf16[768,768]{1,0:T(8,128)(2,1)} %bitcast.5, bf16[16,48,384]{2,1,0:T(8,128)(2,1)S(1)} %bitcast.3, bf16[384,384]{1,0:T(8,128)(2,1)S(1)} %bitcast.4, bf16[384,384]{1,0:T(8,128)(2,1)S(1)} %copy-done.2), custom_call_target="tpu_custom_call" | custom-call | flops 10000000000 | bytes 100000000 | tf_op jit(solution)/shard_map/pallas_call | solution.py:592
  172.2 0.9 copy.9
  173.0 1.0 copy.10
Async XLA Ops:
  1.4 1.1 copy-start
  2.5 1.0 copy-start.1
  3.4 1.0 copy-start.2
